TPU v7x, 128 devices: a whole 4x4x4 slice. The times are simulated.
128 devices in a mesh: wide: 16 (over z, y_lo, core), col: 8 (over y_hi, x).
Axes of the slice: x: 4, y: 4 (y_hi: 2, y_lo: 2; y = y_hi * 2 + y_lo), z: 4, core: 2. Of those that a mesh axis runs over, the one named last changes fastest.
Arguments:
- amplitudes: bfloat16 [1280, 65536], P('col', 'wide'), may hold values from -6 to 6
- integrals: bfloat16 [16, 16, 256, 12288], P(None, 'wide', None, 'col'), may hold values from -0.0234375 to 0.0234375
- tile_rows: int32 [256], replicated, may hold values from 64 to 256, as said below
Outputs:
- ladder: float32 [1280, 12288], P('wide', 'col')
Inputs may be any that keep to these rules, and one draw needn't show every extreme that they name: `tile_rows`: tile 0 is full.
All inputs are finite; a program needn't handle non-finite values.
Results may differ from a plain program's by a relative error of at most 0.0003.
Values may be sent and summed in bfloat16 or wider, within the bound.
A program may use at most 128 MiB of HBM per device.

v0:
```python
import jax
import jax.numpy as jnp
from jax import lax
from jax.sharding import PartitionSpec as P


def shards(amplitudes, integrals, tile_rows):
    width = lax.axis_size("wide")
    tiles = integrals.shape[0]
    tile = integrals.shape[2]
    per_src = tiles // width
    own = lax.axis_index("wide")
    counts = lax.dynamic_slice_in_dim(tile_rows.reshape(tiles, width), own, 1, 1)
    live = (jnp.arange(tile, dtype=jnp.int32)[None, None, :] < counts.T[:, :, None]).astype(
        jnp.bfloat16
    )
    whole = lax.all_gather(amplitudes, "col", axis=0, tiled=True)
    split = whole.reshape(whole.shape[0], per_src, width, tile)
    panel = lax.all_to_all(split, "wide", split_axis=2, concat_axis=2, tiled=True)
    panel = panel * live[None]
    share = panel.shape[0] // width
    summed = lax.psum(
        jnp.einsum("mqsk,sqkn->mn", panel, integrals, preferred_element_type=jnp.float32), "wide"
    )
    return lax.dynamic_slice_in_dim(summed, own * share, share, 0)


def solution(mesh):
    return jax.shard_map(
        shards,
        mesh=mesh,
        in_specs=(P("col", "wide"), P(None, "wide", None, "col"), P()),
        out_specs=P("wide", "col"),
        check_vma=False,
    )
```

profile of v0, /device:TPU:8, one launch (start us, length us, event | category | flops | bytes accessed | tf_op | source)
XLA Modules:
  0.0 501.7 jit_solution(12715620391484931638)
XLA Ops:
  6.5 0.0 all-gather.2.cloned.1.call-start
  6.5 0.7 all-gather.2.cloned.1.call-update
  7.3 132.0 %all-gather.2.cloned.1.call-done = bf16[1280,4096]{1,0:T(8,128)(2,1)} async-done(((bf16[160,4096]{1,0:T(8,128)(2,1)}), bf16[1280,4096]{1,0:T(8,128)(2,1)}) %all-gather.2.cloned.1.call-update) | async-done | bytes 10485776 | tf_op jit(solution)/shard_map/all_gather | solution.py:17
  139.2 14.3 %copy.9 = bf16[1280,4096]{0,1:T(8,128)(2,1)} copy(bf16[1280,4096]{1,0:T(8,128)(2,1)} %all-gather.2.cloned.1.call-done) | data formatting | bytes 20971520 | tf_op jit(solution)/shard_map/all_gather | solution.py:17
  153.5 15.1 %copy.10 = bf16[1280,1,16,256]{3,0,1,2:T(8,128)(2,1)} copy(bf16[1280,1,16,256]{0,3,2,1:T(8,128)(2,1)} %bitcast.13) | data formatting | bytes 20971520 | tf_op jit(solution)/shard_map/reshape | solution.py:18
  168.6 0.0 copy-start
  168.6 6.1 %all-to-all-start = ((bf16[1280,1,16,256]{3,0,1,2:T(8,128)(2,1)}), bf16[1280,1,16,256]{3,0,1,2:T(8,128)(2,1)}, u32[]{:S(2)}, u32[]{:S(2)}) async-start(bf16[1280,1,16,256]{3,0,1,2:T(8,128)(2,1)} %copy.10), calls=%async_computation | async-start | bytes 20971520 | tf_op jit(solution)/shard_map/all_to_all | solution.py:19
  174.8 0.0 all-reduce.2.cloned.1.call-start
  174.8 0.0 copy-done
  174.8 0.1 reshape.46
  174.9 0.2 dynamic-slice_reduce_fusion
  175.1 0.1 fusion.10
  175.2 116.3 %all-to-all-done = bf16[1280,1,16,256]{3,0,1,2:T(8,128)(2,1)} async-done(((bf16[1280,1,16,256]{3,0,1,2:T(8,128)(2,1)}), bf16[1280,1,16,256]{3,0,1,2:T(8,128)(2,1)}, u32[]{:S(2)}, u32[]{:S(2)}) %all-to-all-start) | async-done | bytes 10485792 | tf_op jit(solution)/shard_map/all_to_all | solution.py:19
  291.4 23.8 %fusion.4 = f32[1280,1536]{1,0:T(8,128)} fusion(bf16[16,1,256,1536]{3,2,1,0:T(8,128)(2,1)} %param.4, bf16[1280,1,16,256]{3,0,1,2:T(8,128)(2,1)} %all-to-all-done, bf16[16,256]{1,0:T(8,128)(2,1)S(1)} %fusion.10), kind=kOutput, calls=%fused_computation.4 | convolution fusion | flops 16111370240 | bytes 30941184 | tf_op jit(solution)/shard_map/mqsk,sqkn->mn/dot_general | solution.py:23
  315.2 0.0 all-reduce.2.cloned.1.call-update
  315.2 177.8 %all-reduce.2.cloned.1.call-done = f32[1280,1536]{1,0:T(8,128)} async-done(((f32[1280,1536]{1,0:T(8,128)}), f32[1280,1536]{1,0:T(8,128)}) %all-reduce.2.cloned.1.call-update) | async-done | bytes 7864336 | tf_op jit(solution)/shard_map/psum | solution.py:22
  493.0 1.8 constant_dynamic-slice_fusion
Async XLA Ops:
  6.5 132.7 %all-gather.2.cloned.1.call-start = ((), (), s32[]{:S(2)}) async-start(), calls=%async_computation.1 | async-start | bytes 11796480 | tf_op jit(solution)/shard_map/all_gather | solution.py:17
  168.6 6.2 %copy-start = (s32[256]{0:T(256)S(1)}, s32[256]{0:T(256)}, u32[]{:S(2)}) copy-start(s32[256]{0:T(256)} %param.5) | copy-start | bytes 3076
  168.6 122.8 %all-to-all-start = ((bf16[1280,1,16,256]{3,0,1,2:T(8,128)(2,1)}), bf16[1280,1,16,256]{3,0,1,2:T(8,128)(2,1)}, u32[]{:S(2)}, u32[]{:S(2)}) async-start(bf16[1280,1,16,256]{3,0,1,2:T(8,128)(2,1)} %copy.10), calls=%async_computation | async-start | bytes 20971520 | tf_op jit(solution)/shard_map/all_to_all | solution.py:19
  174.8 318.3 %all-reduce.2.cloned.1.call-start = ((), (), s32[]{:S(2)}) async-start(), calls=%async_computation.2 | async-start | bytes 15728640 | tf_op jit(solution)/shard_map/psum | solution.py:22
Sparse Core Ops, SparseCore 0:
  9.7 129.4 all-gather.1
  315.3 177.6 all-reduce.1
where the time goes:
time: 507 us; the launch traced here: 502 us
  waiting for transfers between devices  427 us (84%)
  local copies, waits for them, and re-layouts  31.5 us (6%)
  matrix products  23.8 us (5%)
  between operations  13.4 us (3%)
  starting transfers between devices  6.18 us (1%)
    psum x1, waiting for transfers between devices, shards(): lax.psum(jnp.einsum('mqsk,sqkn->mn', panel, integrals, preferred_element_...  178 us
    all_gather x1, waiting for transfers between devices, shards(): whole = lax.all_gather(amplitudes, 'col', axis=0, tiled=True)  132 us
    all_to_all x1, waiting for transfers between devices, shards(): lax.all_to_all(split, 'wide', split_axis=2, concat_axis=2, tiled=True)  116 us
    dot_general x1, matrix products, shards(): jnp.einsum('mqsk,sqkn->mn', panel, integrals, preferred_element_type=jnp....  23.8 us
    reshape x1, local copies, waits for them, and re-layouts, shards(): split = whole.reshape(whole.shape[0], per_src, width, tile)  15.1 us
    all_gather x1, local copies, waits for them, and re-layouts, shards(): whole = lax.all_gather(amplitudes, 'col', axis=0, tiled=True)  14.3 us
  transfers between devices with their start and end apart: 3, of which 3 were waited for; matrix products, arithmetic and copies ran while one was open for 0% of the time, Pallas kernels for 0%

commit v1 on v0

v1 whole, which is shorter than its diff:
```python
import functools

import jax
import jax.numpy as jnp
from jax import lax
from jax.experimental import pallas as pl
from jax.experimental.pallas import tpu as pltpu
from jax.sharding import PartitionSpec as P

MESH = pl.DeviceIdType.MESH
SUB = 16
TILE = 256
TILES = 16
N_WIDE = 16
COLS = 8
BLOCK_N = 256


def kernel(
    chunks,
    counts_ref,
    amps_ref,
    ints_ref,
    out_ref,
    panel,
    flat,
    part,
    from_core,
    from_z,
    from_y,
    acc,
    own_sem,
    load_sem,
    a2a_send,
    a2a_recv,
    col_send,
    col_recv,
    red_send,
    red_recv,
):
    wide = lax.axis_index("wide")
    col = lax.axis_index("col")
    z, ylo, core = wide // 4, lax.rem(wide // 2, 2), lax.rem(wide, 2)
    yhi, x = col // 4, lax.rem(col, 4)

    def at_col(dy, dx):
        return lax.rem(yhi + dy, 2) * 4 + lax.rem(x + dx + 4, 4)

    def at_wide(dz, dy, dk):
        return lax.rem(z + dz + 4, 4) * 4 + lax.rem(ylo + dy, 2) * 2 + lax.rem(core + dk, 2)

    def peer(i):
        return lax.rem(z + i // 4, 4) * 4 + lax.rem(ylo + (i // 2) % 2, 2) * 2 + lax.rem(core + i % 2, 2)

    load = pltpu.make_async_copy(ints_ref, flat, load_sem)
    load.start()

    barrier = pltpu.get_barrier_semaphore()
    for i in range(1, N_WIDE):
        pl.semaphore_signal(barrier, 1, device_id=(peer(i), col), device_id_type=MESH)
    for c in (at_col(1, 0), at_col(0, 1), at_col(0, -1)):
        pl.semaphore_signal(barrier, 1, device_id=(wide, c), device_id_type=MESH)
    pl.semaphore_wait(barrier, N_WIDE - 1 + 3)

    def a2a_copy(t, i):
        to = peer(i)
        return pltpu.make_async_remote_copy(
            amps_ref.at[:, pl.ds(pl.multiple_of(t * SUB, SUB), SUB), pl.ds(pl.multiple_of(to * TILE, TILE), TILE)],
            panel.at[t, :, col, :, pl.ds(pl.multiple_of(wide * TILE, TILE), TILE)],
            a2a_send.at[t],
            a2a_recv.at[t],
            device_id=(to, col),
            device_id_type=MESH,
        )

    def own_copy(t):
        return pltpu.make_async_copy(
            amps_ref.at[:, pl.ds(pl.multiple_of(t * SUB, SUB), SUB), pl.ds(pl.multiple_of(wide * TILE, TILE), TILE)],
            panel.at[t, :, col, :, pl.ds(pl.multiple_of(wide * TILE, TILE), TILE)],
            own_sem.at[t],
        )

    def others(t):
        return panel.at[t, :, col, :, pl.ds(0, (N_WIDE - 1) * TILE)]

    def col_copy(t, slot):
        whole = lambda c: panel.at[t, :, c]
        half = lambda c, k: panel.at[t, k, c]
        ref, to = {
            0: lambda: (whole(col), at_col(1, 0)),
            1: lambda: (whole(col), at_col(0, 1)),
            2: lambda: (whole(col), at_col(0, -1)),
            3: lambda: (whole(at_col(1, 0)), at_col(0, 1)),
            4: lambda: (whole(at_col(1, 0)), at_col(0, -1)),
            5: lambda: (half(at_col(0, -1), 0), at_col(0, 1)),
            6: lambda: (half(at_col(0, 1), 1), at_col(0, -1)),
            7: lambda: (half(at_col(1, -1), 0), at_col(0, 1)),
            8: lambda: (half(at_col(1, 1), 1), at_col(0, -1)),
        }[slot]()
        return pltpu.make_async_remote_copy(
            ref, ref, col_send.at[t, slot], col_recv.at[t, slot], device_id=(wide, to), device_id_type=MESH
        )

    def core_copy(t):
        return pltpu.make_async_remote_copy(
            part.at[t, 1 - core],
            from_core.at[t],
            red_send.at[t, 0],
            red_recv.at[t, 0],
            device_id=(at_wide(0, 0, 1), col),
            device_id_type=MESH,
        )

    def z_copy(t, d):
        zo = lax.rem(z + d, 4)
        return pltpu.make_async_remote_copy(
            part.at[t, core, pl.ds(pl.multiple_of(zo * 2 * SUB, 2 * SUB), 2 * SUB)],
            from_z.at[t, d - 1],
            red_send.at[t, d],
            red_recv.at[t, d],
            device_id=(at_wide(d, 0, 0), col),
            device_id_type=MESH,
        )

    def y_copy(t):
        return pltpu.make_async_remote_copy(
            acc.at[t, 1 - ylo],
            from_y.at[t],
            red_send.at[t, 4],
            red_recv.at[t, 4],
            device_id=(at_wide(0, 1, 0), col),
            device_id_type=MESH,
        )

    def scatter(t):
        for i in range(1, N_WIDE):
            a2a_copy(t, i).start()
        own_copy(t).start()

    def mask_and_send(t):
        own_copy(t).wait()
        pltpu.make_async_copy(others(t), others(t), a2a_recv.at[t]).wait()
        for s in range(TILES):
            count = counts_ref[s * N_WIDE + wide]
            where = (t, slice(None), col, slice(None), slice(s * TILE, (s + 1) * TILE))
            live = lax.broadcasted_iota(jnp.int32, (2, SUB, TILE), 2) < count
            panel[where] = jnp.where(live, panel[where].astype(jnp.float32), 0.0).astype(jnp.bfloat16)
        for slot in (0, 1, 2):
            col_copy(t, slot).start()

    def matmul(t):

        @pl.loop(0, flat.shape[1] // BLOCK_N)
        def _(n):
            cols = pl.ds(pl.multiple_of(n * BLOCK_N, BLOCK_N), BLOCK_N)
            left = panel[t].reshape(2 * COLS * SUB, panel.shape[-1])
            res = jnp.dot(left, flat[:, cols], preferred_element_type=jnp.float32)
            part[t, :, :, cols] = res.reshape(2, COLS * SUB, BLOCK_N)

    def gathered(t):
        for slot in (5, 6, 7, 8):
            col_copy(t, slot).wait_recv()

    def core_sum(t):
        core_copy(t).wait_recv()
        part[t, core] = part[t, core] + from_core[t]
        for d in (2, 1, 3):
            z_copy(t, d).start()

    def z_sum(t):
        for d in (1, 2, 3):
            z_copy(t, d).wait_recv()
        rows = pl.ds(pl.multiple_of(z * 2 * SUB, 2 * SUB), 2 * SUB)
        total = part[t, core, rows] + from_z[t, 0] + from_z[t, 1] + from_z[t, 2]
        acc[t] = total.reshape(acc.shape[1:])
        y_copy(t).start()

    def y_sum(t):
        y_copy(t).wait_recv()
        out_ref[pl.ds(pl.multiple_of(t * SUB, SUB), SUB)] = acc[t, ylo] + from_y[t]

    scatter(0)
    scatter(1)
    mask_and_send(0)
    load.wait()

    @pl.loop(0, chunks + 1)
    def _(t):
        @pl.when(t < chunks)
        def _():
            col_copy(t, 0).wait_recv()
            col_copy(t, 3).start()
            col_copy(t, 4).start()
            col_copy(t, 1).wait_recv()
            col_copy(t, 5).start()
            col_copy(t, 2).wait_recv()
            col_copy(t, 6).start()

        @pl.when(t + 1 < chunks)
        def _():
            mask_and_send(t + 1)

        @pl.when(t + 2 < chunks)
        def _():
            scatter(t + 2)

        @pl.when(t >= 1)
        def _():
            gathered(t - 1)
            matmul(t - 1)
            core_copy(t - 1).start()

        @pl.when(t < chunks)
        def _():
            col_copy(t, 3).wait_recv()
            col_copy(t, 7).start()
            col_copy(t, 4).wait_recv()
            col_copy(t, 8).start()

        @pl.when(t >= 2)
        def _():
            z_sum(t - 2)

        @pl.when(t >= 1)
        def _():
            core_sum(t - 1)

        @pl.when(t >= 2)
        def _():
            y_sum(t - 2)

    z_sum(chunks - 1)
    y_sum(chunks - 1)

    @pl.loop(0, chunks)
    def _(t):
        pltpu.make_async_copy(others(t), others(t), a2a_send.at[t]).wait()
        for slot in range(9):
            col_copy(t, slot).wait_send()
        core_copy(t).wait_send()
        for d in (1, 2, 3):
            z_copy(t, d).wait_send()
        y_copy(t).wait_send()


def shards(amplitudes, integrals, tile_rows):
    rows, depth = amplitudes.shape
    chunks = rows // (2 * SUB)
    columns = integrals.shape[-1]
    f32, bf16 = jnp.float32, jnp.bfloat16
    dma = pltpu.SemaphoreType.DMA
    return pl.pallas_call(
        functools.partial(kernel, chunks),
        out_shape=jax.ShapeDtypeStruct((chunks * SUB, columns), f32),
        in_specs=[
            pl.BlockSpec(memory_space=pltpu.SMEM),
            pl.BlockSpec(memory_space=pltpu.VMEM),
            pl.BlockSpec(memory_space=pl.ANY),
        ],
        out_specs=pl.BlockSpec(memory_space=pltpu.VMEM),
        scratch_shapes=[
            pltpu.VMEM((chunks, 2, COLS, SUB, depth), bf16),
            pltpu.VMEM((depth, columns), bf16),
            pltpu.VMEM((chunks, 2, COLS * SUB, columns), f32),
            pltpu.VMEM((chunks, COLS * SUB, columns), f32),
            pltpu.VMEM((chunks, 3, 2 * SUB, columns), f32),
            pltpu.VMEM((chunks, SUB, columns), f32),
            pltpu.VMEM((chunks, 2, SUB, columns), f32),
            dma((chunks,)),
            dma,
            dma((chunks,)),
            dma((chunks,)),
            dma((chunks, 9)),
            dma((chunks, 9)),
            dma((chunks, 5)),
            dma((chunks, 5)),
        ],
        compiler_params=pltpu.CompilerParams(
            collective_id=0, has_side_effects=True, vmem_limit_bytes=60 * 2**20
        ),
        cost_estimate=pl.CostEstimate(
            flops=2 * COLS * rows * depth * columns, bytes_accessed=2 * depth * (rows + columns), transcendentals=0
        ),
        name="ladder",
    )(tile_rows, amplitudes.reshape(2, rows // 2, depth), integrals.reshape(depth, columns))


def solution(mesh):
    return jax.shard_map(
        shards,
        mesh=mesh,
        in_specs=(P("col", "wide"), P(None, "wide", None, "col"), P()),
        out_specs=P("wide", "col"),
        check_vma=False,
    )
```

time: 507 us -> 130 us (0.26)
  waiting for transfers between devices: 427 us -> 0 us
  Pallas kernels: 0 us -> 128 us
  local copies, waits for them, and re-layouts: 31.5 us -> 1.85 us
  matrix products: 23.8 us -> 0 us
  between operations: 13.4 us -> 0.01 us
  starting transfers between devices: 6.18 us -> 0 us
    psum x1 -> x0, waiting for transfers between devices: 178 us -> none  [shards(): lax.psum(jnp.einsum('mqsk,sqkn->mn', panel, integrals, preferred_element_...]
    all_gather x1 -> x0, waiting for transfers between devices: 132 us -> none  [shards(): whole = lax.all_gather(amplitudes, 'col', axis=0, tiled=True)]
    pallas_call x0 -> x1, Pallas kernels: none -> 128 us  [shards(): pl.pallas_call(functools.partial(kernel, chunks), out_shape=jax.ShapeDtyp...]
    all_to_all x1 -> x0, waiting for transfers between devices: 116 us -> none  [shards(): lax.all_to_all(split, 'wide', split_axis=2, concat_axis=2, tiled=True)]
    dot_general x1 -> x0, matrix products: 23.8 us -> none  [shards(): jnp.einsum('mqsk,sqkn->mn', panel, integrals, preferred_element_type=jnp....]
    reshape x2 -> x0, local copies, waits for them, and re-layouts: 15.2 us -> none  [the longest x1 15.1 us: shards(): split = whole.reshape(whole.shape[0], per_src, width, tile)]
    all_gather x1 -> x0, local copies, waits for them, and re-layouts: 14.3 us -> none  [shards(): whole = lax.all_gather(amplitudes, 'col', axis=0, tiled=True)]
    all_to_all x1 -> x0, starting transfers between devices: 6.14 us -> none  [shards(): lax.all_to_all(split, 'wide', split_axis=2, concat_axis=2, tiled=True)]
  transfers between devices with their start and end apart: 3 -> 0, of which waited for: 3 -> 0; matrix products, arithmetic and copies ran while one was open for 0% -> 0% of each run, Pallas kernels for 0% -> 0%
where the time goes in v1:
time: 130 us
  Pallas kernels  128 us (98%)
  local copies, waits for them, and re-layouts  1.85 us (1%)
    pallas_call x1, Pallas kernels, shards(): pl.pallas_call(functools.partial(kernel, chunks), out_shape=jax.ShapeDtyp...  128 us

profile of v1, /device:TPU:8, one launch (start us, length us, event | category | flops | bytes accessed | tf_op | source)
XLA Modules:
  0.0 129.6 jit_solution(2849344838861119446)
XLA Ops:
  0.0 127.7 %ladder.1 = f32[80,1536]{1,0:T(8,128)} custom-call(s32[256]{0:T(256)} %counts_ref.1, bf16[2,80,4096]{2,1,0:T(8,128)(2,1)} %bitcast.3, bf16[4096,1536]{1,0:T(8,128)(2,1)} %bitcast.2), custom_call_target="tpu_custom_call" | custom-call | flops 16106127360 | bytes 13893632 | tf_op jit(solution)/shard_map/ladder/pallas_call | solution.py:252
  127.7 1.8 %copy.5 = f32[80,1536]{1,0:T(8,128)} copy(f32[80,1536]{1,0:T(8,128)} %ladder.1) | data formatting | bytes 983040

commit v2 on v1

--- a/solution.py
+++ b/solution.py
@@ -14,10 +14,15 @@
 N_WIDE = 16
 COLS = 8
 BLOCK_N = 256
+LANES = 128
+WINDOW = TILE + LANES
+PER_WINDOW = WINDOW // LANES
+WIDTHS = (2944, 3200)
 
 
 def kernel(
     chunks,
+    packed,
     counts_ref,
     amps_ref,
     ints_ref,
@@ -37,7 +42,12 @@
     col_recv,
     red_send,
     red_recv,
+    *pack_refs,
 ):
+    if packed:
+        arrived, raw, windows, offs, picks = pack_refs
+    else:
+        arrived, raw = None, flat
     wide = lax.axis_index("wide")
     col = lax.axis_index("col")
     z, ylo, core = wide // 4, lax.rem(wide // 2, 2), lax.rem(wide, 2)
@@ -52,7 +62,7 @@
     def peer(i):
         return lax.rem(z + i // 4, 4) * 4 + lax.rem(ylo + (i // 2) % 2, 2) * 2 + lax.rem(core + i % 2, 2)
 
-    load = pltpu.make_async_copy(ints_ref, flat, load_sem)
+    load = pltpu.make_async_copy(ints_ref, raw, load_sem)
     load.start()
 
     barrier = pltpu.get_barrier_semaphore()
@@ -62,11 +72,16 @@
         pl.semaphore_signal(barrier, 1, device_id=(wide, c), device_id_type=MESH)
     pl.semaphore_wait(barrier, N_WIDE - 1 + 3)
 
+    def landing(t, cols):
+        if packed:
+            return arrived.at[t, :, :, cols]
+        return panel.at[t, :, col, :, cols]
+
     def a2a_copy(t, i):
         to = peer(i)
         return pltpu.make_async_remote_copy(
             amps_ref.at[:, pl.ds(pl.multiple_of(t * SUB, SUB), SUB), pl.ds(pl.multiple_of(to * TILE, TILE), TILE)],
-            panel.at[t, :, col, :, pl.ds(pl.multiple_of(wide * TILE, TILE), TILE)],
+            landing(t, pl.ds(pl.multiple_of(wide * TILE, TILE), TILE)),
             a2a_send.at[t],
             a2a_recv.at[t],
             device_id=(to, col),
@@ -76,12 +91,12 @@
     def own_copy(t):
         return pltpu.make_async_copy(
             amps_ref.at[:, pl.ds(pl.multiple_of(t * SUB, SUB), SUB), pl.ds(pl.multiple_of(wide * TILE, TILE), TILE)],
-            panel.at[t, :, col, :, pl.ds(pl.multiple_of(wide * TILE, TILE), TILE)],
+            landing(t, pl.ds(pl.multiple_of(wide * TILE, TILE), TILE)),
             own_sem.at[t],
         )
 
     def others(t):
-        return panel.at[t, :, col, :, pl.ds(0, (N_WIDE - 1) * TILE)]
+        return landing(t, pl.ds(0, (N_WIDE - 1) * TILE))
 
     def col_copy(t, slot):
         whole = lambda c: panel.at[t, :, c]
@@ -137,14 +152,64 @@
             a2a_copy(t, i).start()
         own_copy(t).start()
 
+    def count_of(s):
+        return counts_ref[s * N_WIDE + wide]
+
+    def mask(t):
+        for s in range(TILES):
+            where = (t, slice(None), col, slice(None), slice(s * TILE, (s + 1) * TILE))
+            live = lax.broadcasted_iota(jnp.int32, (2, SUB, TILE), 2) < count_of(s)
+            panel[where] = jnp.where(live, panel[where].astype(jnp.float32), 0.0).astype(jnp.bfloat16)
+
+    def plan():
+        start = jnp.int32(0)
+        for s in range(TILES):
+            offs[s] = start
+            start = start + (((count_of(s) + (SUB - 1)) >> 4) << 4)
+        offs[TILES] = start
+        ends = [offs[s + 1] for s in range(TILES)]
+
+        @pl.loop(0, panel.shape[-1] // LANES)
+        def _(q):
+            first = jnp.int32(0)
+            for end in ends:
+                first = first + jnp.where(end <= q * LANES, 1, 0)
+            for d in range(3):
+                s = jnp.minimum(first + d, TILES - 1)
+                valid = (first + d < TILES) & (offs[s] < (q + 1) * LANES)
+                picks[q * 3 + d] = jnp.where(valid, s * PER_WINDOW + q - (offs[s] >> 7), TILES * PER_WINDOW)
+
+        windows[TILES * PER_WINDOW] = jnp.zeros(windows.shape[1:], windows.dtype)
+
+    def pack(t):
+        lane = lax.broadcasted_iota(jnp.int32, (2 * SUB, WINDOW), 1)
+        pad = jnp.zeros((2 * SUB, LANES), jnp.float32)
+        for s in range(TILES):
+            phase = offs[s] & (LANES - 1)
+            tile = arrived[t, :, :, s * TILE : (s + 1) * TILE].astype(jnp.float32).reshape(2 * SUB, TILE)
+            turned = pltpu.roll(jnp.concatenate([tile, pad], axis=1), phase, 1)
+            kept = jnp.where((lane >= phase) & (lane < phase + count_of(s)), turned, 0.0).astype(jnp.bfloat16)
+            for b in range(PER_WINDOW):
+                windows[s * PER_WINDOW + b] = kept[:, b * LANES : (b + 1) * LANES].reshape(2, SUB, LANES)
+        for q in range(panel.shape[-1] // LANES):
+            block = windows[picks[q * 3]] + windows[picks[q * 3 + 1]] + windows[picks[q * 3 + 2]]
+            panel[t, :, col, :, q * LANES : (q + 1) * LANES] = block
+
+    def pack_rows():
+        @functools.partial(lax.fori_loop, 0, flat.shape[0] // SUB, init_val=(jnp.int32(0), jnp.int32(0)))
+        def _(b, at):
+            s, i = at
+            flat[pl.ds(pl.multiple_of(b * SUB, SUB), SUB)] = raw[s * (TILE // SUB) + i]
+            last = i + 1 >= ((count_of(s) + (SUB - 1)) >> 4)
+            return jnp.where(last, jnp.minimum(s + 1, TILES - 1), s), jnp.where(last, 0, i + 1)
+
     def mask_and_send(t):
         own_copy(t).wait()
         pltpu.make_async_copy(others(t), others(t), a2a_recv.at[t]).wait()
-        for s in range(TILES):
-            count = counts_ref[s * N_WIDE + wide]
-            where = (t, slice(None), col, slice(None), slice(s * TILE, (s + 1) * TILE))
-            live = lax.broadcasted_iota(jnp.int32, (2, SUB, TILE), 2) < count
-            panel[where] = jnp.where(live, panel[where].astype(jnp.float32), 0.0).astype(jnp.bfloat16)
+        if packed:
+            pack(t)
+        else:
+            mask(t)
         for slot in (0, 1, 2):
             col_copy(t, slot).start()
 
@@ -181,8 +246,12 @@
 
     scatter(0)
     scatter(1)
+    if packed:
+        plan()
     mask_and_send(0)
     load.wait()
+    if packed:
+        pack_rows()
 
     @pl.loop(0, chunks + 1)
     def _(t):
@@ -243,15 +312,25 @@
         y_copy(t).wait_send()
 
 
-def shards(amplitudes, integrals, tile_rows):
-    rows, depth = amplitudes.shape
-    chunks = rows // (2 * SUB)
+def ladder(index, width, amplitudes, integrals, tile_rows):
+    _, rows, depth = amplitudes.shape
+    chunks = rows // SUB
     columns = integrals.shape[-1]
+    packed = width < depth
     f32, bf16 = jnp.float32, jnp.bfloat16
     dma = pltpu.SemaphoreType.DMA
+    pack_scratch = [
+        pltpu.VMEM((chunks, 2, SUB, depth), bf16),
+        pltpu.VMEM((depth // SUB, SUB, columns), bf16),
+        pltpu.VMEM((TILES * PER_WINDOW + 1, 2, SUB, LANES), bf16),
+        pltpu.SMEM((TILES + 1,), jnp.int32),
+        pltpu.SMEM((3 * width // LANES,), jnp.int32),
+    ]
+    if packed:
+        integrals = integrals.reshape(depth // SUB, SUB, columns)
     return pl.pallas_call(
-        functools.partial(kernel, chunks),
-        out_shape=jax.ShapeDtypeStruct((chunks * SUB, columns), f32),
+        functools.partial(kernel, chunks, packed),
+        out_shape=jax.ShapeDtypeStruct((rows, columns), f32),
         in_specs=[
             pl.BlockSpec(memory_space=pltpu.SMEM),
             pl.BlockSpec(memory_space=pltpu.VMEM),
@@ -259,8 +338,8 @@
         ],
         out_specs=pl.BlockSpec(memory_space=pltpu.VMEM),
         scratch_shapes=[
-            pltpu.VMEM((chunks, 2, COLS, SUB, depth), bf16),
-            pltpu.VMEM((depth, columns), bf16),
+            pltpu.VMEM((chunks, 2, COLS, SUB, width), bf16),
+            pltpu.VMEM((width, columns), bf16),
             pltpu.VMEM((chunks, 2, COLS * SUB, columns), f32),
             pltpu.VMEM((chunks, COLS * SUB, columns), f32),
             pltpu.VMEM((chunks, 3, 2 * SUB, columns), f32),
@@ -274,15 +353,30 @@
             dma((chunks, 9)),
             dma((chunks, 5)),
             dma((chunks, 5)),
+            *(pack_scratch if packed else []),
         ],
         compiler_params=pltpu.CompilerParams(
-            collective_id=0, has_side_effects=True, vmem_limit_bytes=60 * 2**20
+            collective_id=index, has_side_effects=True, vmem_limit_bytes=60 * 2**20
         ),
         cost_estimate=pl.CostEstimate(
-            flops=2 * COLS * rows * depth * columns, bytes_accessed=2 * depth * (rows + columns), transcendentals=0
+            flops=4 * COLS * rows * width * columns,
+            bytes_accessed=2 * depth * (2 * rows + columns),
+            transcendentals=0,
         ),
-        name="ladder",
-    )(tile_rows, amplitudes.reshape(2, rows // 2, depth), integrals.reshape(depth, columns))
+        name=f"ladder_{width}",
+    )(tile_rows, amplitudes, integrals)
+
+
+def shards(amplitudes, integrals, tile_rows):
+    rows, depth = amplitudes.shape
+    amplitudes = amplitudes.reshape(2, rows // 2, depth)
+    integrals = integrals.reshape(depth, integrals.shape[-1])
+    padded = (tile_rows + (SUB - 1)) // SUB * SUB
+    need = jnp.max(jnp.sum(padded.reshape(TILES, N_WIDE), axis=0))
+    widths = (*WIDTHS, depth)
+    which = sum((need > width).astype(jnp.int32) for width in WIDTHS)
+    branches = [functools.partial(ladder, i, width) for i, width in enumerate(widths)]
+    return lax.switch(which, branches, amplitudes, integrals, tile_rows)
 
 
 def solution(mesh):

time: 130 us -> 113 us (0.87)
  Pallas kernels: 128 us -> 110 us
  other arithmetic: 0 us -> 1.35 us
  between operations: 0.01 us -> 1.31 us
    pallas_call x1, Pallas kernels: 128 us -> 110 us  [ladder(): pl.pallas_call(functools.partial(kernel, chunks, packed), out_shape=jax.S...]
where the time goes in v2:
time: 113 us
  Pallas kernels  110 us (97%)
  other arithmetic  1.35 us (1%)
  between operations  1.31 us (1%)
    pallas_call x1, Pallas kernels, ladder(): pl.pallas_call(functools.partial(kernel, chunks, packed), out_shape=jax.S...  110 us

profile of v2, /device:TPU:8, one launch (start us, length us, event | category | flops | bytes accessed | tf_op | source)
XLA Modules:
  0.0 113.1 jit_solution(14045043551670177878)
XLA Ops:
  0.0 0.7 fusion
  0.7 0.1 reshape.9
  0.8 0.6 reduce_max.9
  2.7 109.6 %conditional.1 = (f32[80,1536]{1,0:T(8,128)S(1)}) conditional(s32[]{:T(128)} %clamp.3, (bf16[16,1,256,1536]{3,2,1,0:T(8,128)(2,1)}, s32[256]{0:T(256)}, bf16[2,80,4096]{2,1,0:T(8,128)(2,1)}) %tuple.28, (bf16[16,1,256,1536]{3,2,1,0:T(8,128)(2,1)}, s32[256]{0:T(256)}, bf16[2,80,4096]{2,1,0:T(8,128)(2,1)}) %tuple.29, (s32[256]{0:T(256)}, ...), branch_computations={%region_2.3_spmd, %region_3.4_spmd, %region_4.5_spmd} | conditional | flops 16106127360 | bytes 13893640 | solution.py:379
  2.8 109.6 %ladder_3200.1 = f32[80,1536]{1,0:T(8,128)S(1)} custom-call(s32[256]{0:T(256)} %get-tuple-element.30.counts_ref, bf16[2,80,4096]{2,1,0:T(8,128)(2,1)} %get-tuple-element.31.amps_ref, bf16[256,16,1536]{2,1,0:T(8,128)(2,1)} %bitcast.11), custom_call_target="tpu_custom_call" | custom-call | flops 12582912000 | bytes 13893632 | tf_op jit(solution)/shard_map/cond/branch_1_fun/ladder_3200/pallas_call | solution.py:331
  112.4 0.8 copy.17
  (1 shorter events, 0.0 us)

commit v3 on v2

--- a/solution.py
+++ b/solution.py
@@ -17,7 +17,8 @@
 LANES = 128
 WINDOW = TILE + LANES
 PER_WINDOW = WINDOW // LANES
-WIDTHS = (2944, 3200)
+PIECES = 2
+WIDTHS = (2944, 3072, 3200, 3328)
 
 
 def kernel(
@@ -116,33 +117,33 @@
             ref, ref, col_send.at[t, slot], col_recv.at[t, slot], device_id=(wide, to), device_id_type=MESH
         )
 
-    def core_copy(t):
-        return pltpu.make_async_remote_copy(
-            part.at[t, 1 - core],
-            from_core.at[t],
-            red_send.at[t, 0],
-            red_recv.at[t, 0],
+    def core_copy(t, p):
+        return pltpu.make_async_remote_copy(
+            part.at[t, p, 1 - core],
+            from_core.at[t, p],
+            red_send.at[t, p * 5],
+            red_recv.at[t, p * 5],
             device_id=(at_wide(0, 0, 1), col),
             device_id_type=MESH,
         )
 
-    def z_copy(t, d):
+    def z_copy(t, p, d):
         zo = lax.rem(z + d, 4)
         return pltpu.make_async_remote_copy(
-            part.at[t, core, pl.ds(pl.multiple_of(zo * 2 * SUB, 2 * SUB), 2 * SUB)],
-            from_z.at[t, d - 1],
-            red_send.at[t, d],
-            red_recv.at[t, d],
+            part.at[t, p, core, pl.ds(pl.multiple_of(zo * 2 * SUB, 2 * SUB), 2 * SUB)],
+            from_z.at[t, p, d - 1],
+            red_send.at[t, p * 5 + d],
+            red_recv.at[t, p * 5 + d],
             device_id=(at_wide(d, 0, 0), col),
             device_id_type=MESH,
         )
 
-    def y_copy(t):
-        return pltpu.make_async_remote_copy(
-            acc.at[t, 1 - ylo],
-            from_y.at[t],
-            red_send.at[t, 4],
-            red_recv.at[t, 4],
+    def y_copy(t, p):
+        return pltpu.make_async_remote_copy(
+            acc.at[t, p, 1 - ylo],
+            from_y.at[t, p],
+            red_send.at[t, p * 5 + 4],
+            red_recv.at[t, p * 5 + 4],
             device_id=(at_wide(0, 1, 0), col),
             device_id_type=MESH,
         )
@@ -214,35 +215,40 @@
             col_copy(t, slot).start()
 
     def matmul(t):
-
-        @pl.loop(0, flat.shape[1] // BLOCK_N)
-        def _(n):
-            cols = pl.ds(pl.multiple_of(n * BLOCK_N, BLOCK_N), BLOCK_N)
-            left = panel[t].reshape(2 * COLS * SUB, panel.shape[-1])
-            res = jnp.dot(left, flat[:, cols], preferred_element_type=jnp.float32)
-            part[t, :, :, cols] = res.reshape(2, COLS * SUB, BLOCK_N)
+        left = panel[t].reshape(2 * COLS * SUB, panel.shape[-1])
+        piece = part.shape[-1]
+        for p in range(PIECES):
+            for n in range(0, piece, BLOCK_N):
+                cols = slice(p * piece + n, p * piece + n + BLOCK_N)
+                res = jnp.dot(left, flat[:, cols], preferred_element_type=jnp.float32)
+                part[t, p, :, :, n : n + BLOCK_N] = res.reshape(2, COLS * SUB, BLOCK_N)
+            core_copy(t, p).start()
 
     def gathered(t):
         for slot in (5, 6, 7, 8):
             col_copy(t, slot).wait_recv()
 
     def core_sum(t):
-        core_copy(t).wait_recv()
-        part[t, core] = part[t, core] + from_core[t]
-        for d in (2, 1, 3):
-            z_copy(t, d).start()
+        for p in range(PIECES):
+            core_copy(t, p).wait_recv()
+            part[t, p, core] = part[t, p, core] + from_core[t, p]
+            for d in (2, 1, 3):
+                z_copy(t, p, d).start()
 
     def z_sum(t):
-        for d in (1, 2, 3):
-            z_copy(t, d).wait_recv()
         rows = pl.ds(pl.multiple_of(z * 2 * SUB, 2 * SUB), 2 * SUB)
-        total = part[t, core, rows] + from_z[t, 0] + from_z[t, 1] + from_z[t, 2]
-        acc[t] = total.reshape(acc.shape[1:])
-        y_copy(t).start()
+        for p in range(PIECES):
+            for d in (1, 2, 3):
+                z_copy(t, p, d).wait_recv()
+            total = part[t, p, core, rows] + from_z[t, p, 0] + from_z[t, p, 1] + from_z[t, p, 2]
+            acc[t, p] = total.reshape(acc.shape[2:])
+            y_copy(t, p).start()
 
     def y_sum(t):
-        y_copy(t).wait_recv()
-        out_ref[pl.ds(pl.multiple_of(t * SUB, SUB), SUB)] = acc[t, ylo] + from_y[t]
+        piece = part.shape[-1]
+        for p in range(PIECES):
+            y_copy(t, p).wait_recv()
+            out_ref[pl.ds(pl.multiple_of(t * SUB, SUB), SUB), p * piece : (p + 1) * piece] = acc[t, p, ylo] + from_y[t, p]
 
     scatter(0)
     scatter(1)
@@ -277,7 +283,6 @@
         def _():
             gathered(t - 1)
             matmul(t - 1)
-            core_copy(t - 1).start()
 
         @pl.when(t < chunks)
         def _():
@@ -286,19 +291,20 @@
             col_copy(t, 4).wait_recv()
             col_copy(t, 8).start()
 
+        @pl.when(t >= 1)
+        def _():
+            core_sum(t - 1)
+
         @pl.when(t >= 2)
         def _():
             z_sum(t - 2)
 
-        @pl.when(t >= 1)
-        def _():
-            core_sum(t - 1)
-
-        @pl.when(t >= 2)
-        def _():
-            y_sum(t - 2)
+        @pl.when(t >= 3)
+        def _():
+            y_sum(t - 3)
 
     z_sum(chunks - 1)
+    y_sum(chunks - 2)
     y_sum(chunks - 1)
 
     @pl.loop(0, chunks)
@@ -306,16 +312,18 @@
         pltpu.make_async_copy(others(t), others(t), a2a_send.at[t]).wait()
         for slot in range(9):
             col_copy(t, slot).wait_send()
-        core_copy(t).wait_send()
-        for d in (1, 2, 3):
-            z_copy(t, d).wait_send()
-        y_copy(t).wait_send()
+        for p in range(PIECES):
+            core_copy(t, p).wait_send()
+            for d in (1, 2, 3):
+                z_copy(t, p, d).wait_send()
+            y_copy(t, p).wait_send()
 
 
 def ladder(index, width, amplitudes, integrals, tile_rows):
     _, rows, depth = amplitudes.shape
     chunks = rows // SUB
     columns = integrals.shape[-1]
+    piece = columns // PIECES
     packed = width < depth
     f32, bf16 = jnp.float32, jnp.bfloat16
     dma = pltpu.SemaphoreType.DMA
@@ -340,19 +348,19 @@
         scratch_shapes=[
             pltpu.VMEM((chunks, 2, COLS, SUB, width), bf16),
             pltpu.VMEM((width, columns), bf16),
-            pltpu.VMEM((chunks, 2, COLS * SUB, columns), f32),
-            pltpu.VMEM((chunks, COLS * SUB, columns), f32),
-            pltpu.VMEM((chunks, 3, 2 * SUB, columns), f32),
-            pltpu.VMEM((chunks, SUB, columns), f32),
-            pltpu.VMEM((chunks, 2, SUB, columns), f32),
+            pltpu.VMEM((chunks, PIECES, 2, COLS * SUB, piece), f32),
+            pltpu.VMEM((chunks, PIECES, COLS * SUB, piece), f32),
+            pltpu.VMEM((chunks, PIECES, 3, 2 * SUB, piece), f32),
+            pltpu.VMEM((chunks, PIECES, SUB, piece), f32),
+            pltpu.VMEM((chunks, PIECES, 2, SUB, piece), f32),
             dma((chunks,)),
             dma,
             dma((chunks,)),
             dma((chunks,)),
             dma((chunks, 9)),
             dma((chunks, 9)),
-            dma((chunks, 5)),
-            dma((chunks, 5)),
+            dma((chunks, 5 * PIECES)),
+            dma((chunks, 5 * PIECES)),
             *(pack_scratch if packed else []),
         ],
         compiler_params=pltpu.CompilerParams(

time: 113 us -> 111 us (0.982)
  Pallas kernels: 110 us -> 106 us
  between operations: 1.31 us -> 2.61 us
    pallas_call x1, Pallas kernels: 110 us -> 106 us  [ladder(): pl.pallas_call(functools.partial(kernel, chunks, packed), out_shape=jax.S...]
where the time goes in v3:
time: 111 us
  Pallas kernels  106 us (95%)
  between operations  2.61 us (2%)
  other arithmetic  1.35 us (1%)
    pallas_call x1, Pallas kernels, ladder(): pl.pallas_call(functools.partial(kernel, chunks, packed), out_shape=jax.S...  106 us

profile of v3, /device:TPU:8, one launch (start us, length us, event | category | flops | bytes accessed | tf_op | source)
XLA Modules:
  0.0 111.0 jit_solution(385851992015911925)
XLA Ops:
  0.0 0.7 fusion
  0.7 0.1 reshape.9
  0.8 0.6 reduce_max.9
  4.0 106.2 %conditional.1 = (f32[80,1536]{1,0:T(8,128)S(1)}) conditional(s32[]{:T(128)} %clamp.3, (bf16[16,1,256,1536]{3,2,1,0:T(8,128)(2,1)}, s32[256]{0:T(256)}, bf16[2,80,4096]{2,1,0:T(8,128)(2,1)}) %tuple.42, (bf16[16,1,256,1536]{3,2,1,0:T(8,128)(2,1)}, s32[256]{0:T(256)}, bf16[2,80,4096]{2,1,0:T(8,128)(2,1)}) %tuple.43, ...), branch_computations={%region_2.3_spmd, %region_3.4_spmd, %region_4.5_spmd, %region_5.6_... | conditional | flops 16106127360 | bytes 13893640 | solution.py:387
  4.2 105.8 %ladder_3200.1 = f32[80,1536]{1,0:T(8,128)S(1)} custom-call(s32[256]{0:T(256)} %get-tuple-element.47.counts_ref, bf16[2,80,4096]{2,1,0:T(8,128)(2,1)} %get-tuple-element.48.amps_ref, bf16[256,16,1536]{2,1,0:T(8,128)(2,1)} %bitcast.18), custom_call_target="tpu_custom_call" | custom-call | flops 12582912000 | bytes 13893632 | tf_op jit(solution)/shard_map/cond/branch_2_fun/ladder_3200/pallas_call | solution.py:339
  110.2 0.8 copy.25
  (1 shorter events, 0.0 us)
